TPU v7x, 128 devices: a whole 4x4x4 slice. The times are simulated.
128 devices in a mesh: cfg: 2 (over z_hi), tm: 8 (over z_lo, x), height: 8 (over y, core).
Axes of the slice: x: 4, y: 4, z: 4 (z_hi: 2, z_lo: 2; z = z_hi * 2 + z_lo), core: 2. Of those that a mesh axis runs over, the one named last changes fastest.
Arguments:
- query: bfloat16 [2, 8, 8, 1, 384, 1536], P('cfg', 'tm', 'height'), may hold values from -6.5 to 6.5
- keyval: bfloat16 [2, 2, 8, 8, 1, 384, 1536], P(None, 'cfg', 'tm', 'height'), may hold values from -6.5 to 6.5
- hidden: bfloat16 [2, 8, 8, 1, 384, 3072], P('cfg', 'tm', 'height'), may hold values from -3 to 3
- out_weight: bfloat16 [1536, 3072], replicated, may hold values from -0.15625 to 0.15625
- gate_scale: float32 [2, 3072], P('cfg'), may hold values from 0.5 to 2
- guidance: float32 [1], replicated, may hold values from 1.5 to 4
- counts: int32 [8, 8, 1], replicated, may hold values from 192 to 384, as said below
Outputs:
- guided: bfloat16 [8, 8, 1, 384, 3072], P('tm', 'height', None, None, 'cfg')
Inputs may be any that keep to these rules, and one draw needn't show every extreme that they name: `counts`: A tile's valid tokens are its first ones; every tile outside the last time tile and the last height tile has 384.
All inputs are finite; a program needn't handle non-finite values.
Results may differ from a plain program's by a relative error of at most 0.011.
Values may be sent and summed in bfloat16 or wider, within the bound.
A program may use at most 192 MiB of HBM per device.

v0:
```python
import jax
import jax.numpy as jnp
import numpy as np
from jax import lax
from jax.sharding import PartitionSpec as P

HEAD_DIM = 128


head_pair = 2
masked_score = -1e30


def with_halo(shard, sides, width):
    for axis, dim in sides:
        size, length = (lax.axis_size(axis), shard.shape[dim])
        up = [(i, (i + 1) % size) for i in range(size - 1)]
        down = [(j, i) for i, j in up]
        last = lax.slice_in_dim(shard, length - width, length, axis=dim)
        first = lax.slice_in_dim(shard, 0, width, axis=dim)
        before = lax.ppermute(last, axis, up)
        after = lax.ppermute(first, axis, down)
        shard = jnp.concatenate([before, shard, after], axis=dim)
    return shard


def attend_group(query_part, key_part, value_part, key_live, query_live, head_dim):
    width_tiles, tile_rows = (query_part.shape[0], query_part.shape[1])
    queries = query_part.reshape(width_tiles, tile_rows, head_pair, head_dim)
    key_rows = key_part.reshape(width_tiles, -1, head_pair, head_dim)
    value_rows = value_part.reshape(width_tiles, -1, head_pair, head_dim)
    scores = jnp.einsum(
        "wqhd,wkhd->whqk", queries, key_rows, preferred_element_type=jnp.float32
    ) * head_dim ** (-0.5)
    scores = jnp.where(key_live[:, None, None, :], scores, masked_score)
    row_max = jnp.max(scores, axis=-1, keepdims=True)
    exponent = jnp.exp(scores - row_max)
    probs = (exponent / jnp.sum(exponent, axis=-1, keepdims=True)).astype(jnp.bfloat16)
    mixed = jnp.einsum("whqk,wkhd->wqhd", probs, value_rows, preferred_element_type=jnp.float32)
    mixed = mixed * query_live[:, :, None, None]
    return mixed.astype(jnp.bfloat16).reshape(width_tiles, tile_rows, head_pair * head_dim)


def on_device(query, keyval, hidden, out_weight, gate_scale, guidance, counts):
    width_tiles = query.shape[3]
    tile_rows = query.shape[4]
    channels = query.shape[5]
    model_width = hidden.shape[5]
    head_dim = HEAD_DIM
    own_time = lax.axis_index("tm")
    own_height = lax.axis_index("height")
    beside_all = with_halo(keyval, (("tm", 2), ("height", 3)), 1)
    span = min(3, width_tiles)
    starts = [min(max(0 - 1, 0), width_tiles - span)]
    nearby = np.array([[abs(starts[0]) <= 1]])
    slab = jnp.pad(counts, 1)
    slab = lax.dynamic_slice(slab, (own_time, own_height, jnp.int32(0)), (3, 3, width_tiles + 2))
    window_counts = jnp.stack(
        [slab[:, :, start + 1 : start + 1 + span] for start in starts], axis=0
    )
    window_counts = jnp.where(jnp.asarray(nearby)[:, None, None, :], window_counts, 0)
    position = jnp.arange(tile_rows, dtype=jnp.int32)
    key_live = (position[None, None, None, None, :] < window_counts[..., None]).reshape(
        width_tiles, -1
    )
    own_count = slab[1, 1, 1 : 1 + width_tiles]
    query_live = (position[None, :] < own_count[:, None]).astype(jnp.float32)
    windows = jnp.stack([beside_all[:, 0, :, :, start : start + span] for start in starts], axis=1)
    windows = windows.reshape(2, width_tiles, 9 * span * tile_rows, channels)
    own_queries = query.reshape(width_tiles, tile_rows, channels)
    pieces = []
    for head_group in range(channels // (head_pair * head_dim)):
        start_col = head_group * head_pair * head_dim
        stop_col = start_col + head_pair * head_dim
        key_part = windows[0, :, :, start_col:stop_col]
        value_part = windows[1, :, :, start_col:stop_col]
        pieces.append(
            attend_group(
                own_queries[:, :, start_col:stop_col],
                key_part,
                value_part,
                key_live,
                query_live,
                head_dim,
            )
        )
    attended = jnp.concatenate(pieces, axis=-1).reshape(width_tiles * tile_rows, channels)
    projected = jnp.dot(attended, out_weight, preferred_element_type=jnp.float32)
    stream = hidden.reshape(width_tiles * tile_rows, model_width).astype(jnp.float32)
    prediction = (stream + gate_scale[0][None, :] * projected).astype(jnp.bfloat16)
    prediction = prediction.reshape(1, 1, 1, width_tiles, tile_rows, model_width)
    both = lax.all_to_all(prediction, "cfg", split_axis=5, concat_axis=0, tiled=True)
    cond_pred = both[0].astype(jnp.float32)
    uncond_pred = both[1].astype(jnp.float32)
    guided = uncond_pred + guidance[0] * (cond_pred - uncond_pred)
    return guided.astype(jnp.bfloat16)


def solution(mesh):
    return jax.shard_map(
        on_device,
        mesh=mesh,
        in_specs=(
            P("cfg", "tm", "height", None, None, None),
            P(None, "cfg", "tm", "height", None, None, None),
            P("cfg", "tm", "height", None, None, None),
            P(),
            P("cfg", None),
            P(),
            P(),
        ),
        out_specs=P("tm", "height", None, None, "cfg"),
        check_vma=False,
    )
```

profile of v0, /device:TPU:11, one launch (start us, length us, event | category | flops | bytes accessed | tf_op | source)
XLA Modules:
  0.0 413.2 jit_solution(7789672562594169860)
XLA Ops:
  5.6 48.8 %collective-permute-done = bf16[2,1,1,1,1,384,1536]{6,5,3,2,0,4,1:T(8,128)(2,1)S(1)} collective-permute-done((bf16[2,1,1,1,1,384,1536]{6,5,3,2,0,4,1:T(8,128)(2,1)}, bf16[2,1,1,1,1,384,1536]{6,5,3,2,0,4,1:T(8,128)(2,1)S(1)}, u32[]{:S(2)}, u32[]{:S(2)}) %collective-permute-start) | collective-permute-done | bytes 2359328 | tf_op jit(solution)/shard_map/ppermute | solution.py:21
  57.2 5.6 %pad_maximum_fusion.1 = bf16[2,1,3,1,1,384,1536]{6,5,3,2,0,4,1:T(8,128)(2,1)} fusion(bf16[2,1,1,1,1,384,1536]{6,5,3,2,0,4,1:T(8,128)(2,1)S(1)} %collective-permute-done.1, bf16[2,1,1,1,1,384,1536]{6,5,3,2,0,4,1:T(8,128)(2,1)} %bitcast.216, bf16[2,1,1,1,1,384,1536]{6,5,3,2,0,4,1:T(8,128)(2,1)S(1)} %collective-permute-done), kind=kLoop, calls=%fused_computation.43 | loop fusion | flops 7077888 | bytes 14155776 | tf_op jit(solution)/shard_map/concatenate | solution.py:23
  62.8 5.1 %collective-permute-start.2 = (bf16[2,1,3,1,1,384,1536]{6,5,3,2,0,4,1:T(8,128)(2,1)}, bf16[2,1,3,1,1,384,1536]{6,5,3,2,0,4,1:T(8,128)(2,1)}, u32[]{:S(2)}, u32[]{:S(2)}) collective-permute-start(bf16[2,1,3,1,1,384,1536]{6,5,3,2,0,4,1:T(8,128)(2,1)} %pad_maximum_fusion.1), channel_id=1, source_target_pairs={{0,1},{1,2},{2,3},{3,4},{4,5},{5,6},{6,7},{8,9},{9,10},{10,11},{11... | collective-permute-start | bytes 21233672 | tf_op jit(solution)/shard_map/ppermute | solution.py:21
  74.1 70.4 %collective-permute-done.2 = bf16[2,1,3,1,1,384,1536]{6,5,3,2,0,4,1:T(8,128)(2,1)} collective-permute-done((bf16[2,1,3,1,1,384,1536]{6,5,3,2,0,4,1:T(8,128)(2,1)}, bf16[2,1,3,1,1,384,1536]{6,5,3,2,0,4,1:T(8,128)(2,1)}, u32[]{:S(2)}, u32[]{:S(2)}) %collective-permute-start.2) | collective-permute-done | bytes 7077920 | tf_op jit(solution)/shard_map/ppermute | solution.py:21
  144.5 4.4 %collective-permute-done.3 = bf16[2,1,3,1,1,384,1536]{6,5,3,2,0,4,1:T(8,128)(2,1)} collective-permute-done((bf16[2,1,3,1,1,384,1536]{6,5,3,2,0,4,1:T(8,128)(2,1)}, bf16[2,1,3,1,1,384,1536]{6,5,3,2,0,4,1:T(8,128)(2,1)}, u32[]{:S(2)}, u32[]{:S(2)}) %collective-permute-start.3) | collective-permute-done | bytes 7077920 | tf_op jit(solution)/shard_map/ppermute | solution.py:22
  148.9 14.0 %pad_maximum_fusion = bf16[2,1,3,3,1,384,1536]{6,5,3,2,0,4,1:T(8,128)(2,1)} fusion(bf16[2,1,3,1,1,384,1536]{6,5,3,2,0,4,1:T(8,128)(2,1)} %collective-permute-done.3, bf16[2,1,1,1,1,384,1536]{6,5,3,2,0,4,1:T(8,128)(2,1)} %copy-done.3, bf16[2,1,1,1,1,384,1536]{6,5,3,2,0,4,1:T(8,128)(2,1)S(1)} %bitcast.217, ...), kind=kLoop, calls=%fused_computation.6 | loop fusion | flops 42467328 | bytes 42467328 | tf_op jit(solution)/shard_map/concatenate | solution.py:23
  163.0 13.9 %fusion.102 = (bf16[1,1,3456,256]{3,2,0,1:T(8,128)(2,1)}, bf16[1,1,3456,256]{3,2,0,1:T(8,128)(2,1)}, bf16[1,1,3456,256]{3,2,0,1:T(8,128)(2,1)}, bf16[1,1,3456,25...) fusion(bf16[2,1,3456,1536]{3,2,0,1:T(8,128)(2,1)} %bitcast.209), kind=kLoop, calls=%fused_computation.126 | loop fusion | bytes 42467328 | tf_op jit(solution)/shard_map/slice | solution.py:75
  176.9 3.9 copy.144
  180.8 3.9 copy.143
  184.6 3.9 copy.139
  188.5 3.9 copy.138
  192.4 3.9 copy.134
  196.3 3.9 copy.133
  200.2 3.8 copy.129
  204.0 3.9 copy.128
  207.9 3.9 copy.124
  211.8 3.9 copy.123
  220.5 9.0 %fusion.104 = (f32[2,384]{1,0:T(2,128)S(1)}, f32[2,384,3456]{1,2,0:T(8,128)}) fusion(pred[3456]{0:T(1024)(128)(4,1)S(1)} %lt.49, bf16[3456,2,128]{0,2,1:T(8,128)(2,1)S(1)} %bitcast.229, bf16[384,2,128]{0,2,1:T(8,128)(2,1)} %bitcast.236), kind=kOutput, calls=%fused_computation.128 | convolution fusion | flops 690097536 | bytes 12589440 | tf_op jit(solution)/shard_map/sub | solution.py:37
  229.5 5.3 %fusion.76 = bf16[1,2,128,384]{3,2,1,0:T(8,128)(2,1)S(1)} fusion(bf16[3456,2,128]{0,2,1:T(8,128)(2,1)S(1)} %bitcast.230, f32[2,384,3456]{1,2,0:T(8,128)} %get-tuple-element.24, f32[2,384]{1,0:T(2,128)S(1)} %get-tuple-element.23, f32[384]{0:T(512)S(1)} %fusion.89), kind=kOutput, calls=%fused_computation.95 | convolution fusion | flops 684982272 | bytes 12587520 | tf_op jit(solution)/shard_map/whqk,wkhd->wqhd/dot_general | solution.py:39
  235.4 9.0 %fusion.109 = (f32[2,384]{1,0:T(2,128)S(1)}, f32[2,384,3456]{1,2,0:T(8,128)}) fusion(pred[3456]{0:T(1024)(128)(4,1)S(1)} %lt.49, bf16[3456,2,128]{0,2,1:T(8,128)(2,1)S(1)} %bitcast.228, bf16[384,2,128]{0,2,1:T(8,128)(2,1)} %bitcast.235), kind=kOutput, calls=%fused_computation.133 | convolution fusion | flops 690097536 | bytes 12589440 | tf_op jit(solution)/shard_map/sub | solution.py:37
  244.4 9.0 %fusion.108 = (f32[2,384]{1,0:T(2,128)S(1)}, f32[2,384,3456]{1,2,0:T(8,128)}) fusion(pred[3456]{0:T(1024)(128)(4,1)S(1)} %lt.49, bf16[3456,2,128]{0,2,1:T(8,128)(2,1)S(1)} %bitcast.227, bf16[384,2,128]{0,2,1:T(8,128)(2,1)} %bitcast.234), kind=kOutput, calls=%fused_computation.132 | convolution fusion | flops 690097536 | bytes 12589440 | tf_op jit(solution)/shard_map/sub | solution.py:37
  253.5 9.5 %fusion.107 = (f32[2,384]{1,0:T(2,128)}, f32[2,384,3456]{1,2,0:T(8,128)}) fusion(pred[3456]{0:T(1024)(128)(4,1)S(1)} %lt.49, bf16[3456,2,128]{0,2,1:T(8,128)(2,1)S(1)} %bitcast.226, bf16[384,2,128]{0,2,1:T(8,128)(2,1)} %bitcast.233), kind=kOutput, calls=%fused_computation.131 | convolution fusion | flops 690097536 | bytes 12589440 | tf_op jit(solution)/shard_map/sub | solution.py:37
  263.0 9.4 %fusion.106 = (f32[2,384]{1,0:T(2,128)}, f32[2,384,3456]{1,2,0:T(8,128)}) fusion(pred[3456]{0:T(1024)(128)(4,1)S(1)} %lt.49, bf16[3456,2,128]{0,2,1:T(8,128)(2,1)S(1)} %bitcast.225, bf16[384,2,128]{0,2,1:T(8,128)(2,1)} %bitcast.232), kind=kOutput, calls=%fused_computation.130 | convolution fusion | flops 690097536 | bytes 12589440 | tf_op jit(solution)/shard_map/sub | solution.py:37
  272.5 9.9 %fusion.105 = (f32[2,384]{1,0:T(2,128)}, f32[2,384,3456]{1,2,0:T(8,128)}) fusion(pred[3456]{0:T(1024)(128)(4,1)S(1)} %lt.49, bf16[3456,2,128]{0,2,1:T(8,128)(2,1)S(1)} %bitcast.224, bf16[384,2,128]{0,2,1:T(8,128)(2,1)} %bitcast.231), kind=kOutput, calls=%fused_computation.129 | convolution fusion | flops 690097536 | bytes 12589440 | tf_op jit(solution)/shard_map/sub | solution.py:37
  282.5 5.3 %fusion.75 = bf16[1,2,128,384]{3,2,1,0:T(8,128)(2,1)S(1)} fusion(bf16[3456,2,128]{0,2,1:T(8,128)(2,1)S(1)} %bitcast.223, f32[2,384,3456]{1,2,0:T(8,128)} %get-tuple-element.26, f32[2,384]{1,0:T(2,128)} %get-tuple-element.25, f32[384]{0:T(512)S(1)} %fusion.89), kind=kOutput, calls=%fused_computation.94 | convolution fusion | flops 684982272 | bytes 12587520 | tf_op jit(solution)/shard_map/whqk,wkhd->wqhd/dot_general | solution.py:39
  295.6 5.9 %fusion.72 = bf16[1,2,128,384]{3,2,1,0:T(8,128)(2,1)S(1)} fusion(bf16[3456,2,128]{0,2,1:T(8,128)(2,1)S(1)} %bitcast.220, f32[2,384,3456]{1,2,0:T(8,128)} %get-tuple-element.32, f32[2,384]{1,0:T(2,128)S(1)} %get-tuple-element.31, f32[384]{0:T(512)S(1)} %fusion.89), kind=kOutput, calls=%fused_computation.91 | convolution fusion | flops 684982272 | bytes 12587520 | tf_op jit(solution)/shard_map/whqk,wkhd->wqhd/dot_general | solution.py:39
  305.8 4.3 %fusion.55 = bf16[1,1,1,1,384,3072]{5,4,3,2,1,0:T(8,128)(2,1)S(1)} fusion(bf16[1536,3072]{1,0:T(8,128)(2,1)S(1)} %bitcast.245, bf16[1,1,1,1,384,3072]{5,4,3,2,1,0:T(8,128)(2,1)S(1)} %copy-done.18, f32[3072]{0:T(1024)S(1)} %bitcast.246, bf16[1,384,1536]{1,2,0:T(8,128)(2,1)S(1)} %constant_dynamic-update-slice_fusion), kind=kOutput, calls=%fused_computation.70 | convolution fusion | flops 3628597248 | bytes 15347712 | tf_op jit(solution)/shard_map/dot_general | solution.py:88
  310.1 8.1 %copy.148 = bf16[1,1,1,1,384,3072]{4,3,2,1,0,5:T(2,128)(2,1)} copy(bf16[1,1,1,1,384,3072]{5,4,3,2,1,0:T(8,128)(2,1)S(1)} %fusion.55) | data formatting | bytes 4718592 | tf_op jit(solution)/shard_map/reshape | solution.py:91
  318.7 50.8 %reduce.24 = bf16[3072,384]{1,0:T(8,128)(2,1)S(1)} reduce(bf16[3072,1,1,1,1,384]{5,4,3,2,1,0:T(2,128)(2,1)} %bitcast.210, bf16[]{:T(256)} %broadcast.172), dimensions={1,2,3,4}, to_apply=%bitcast.162.reduce_sub_computation | reduce | bytes 4718594
  371.3 4.9 %all-to-all-start = ((bf16[2,2,294912]{2,1,0:T(2,128)(2,1)}), bf16[2,2,294912]{2,1,0:T(2,128)(2,1)S(1)}, u32[]{:S(2)}, u32[]{:S(2)}) async-start(bf16[2,2,294912]{2,1,0:T(2,128)(2,1)} %reshape.353), calls=%async_computation | async-start | bytes 4718592 | tf_op jit(solution)/shard_map/all_to_all | solution.py:92
  376.8 28.2 %all-to-all-done = bf16[2,2,294912]{2,1,0:T(2,128)(2,1)S(1)} async-done(((bf16[2,2,294912]{2,1,0:T(2,128)(2,1)}), bf16[2,2,294912]{2,1,0:T(2,128)(2,1)S(1)}, u32[]{:S(2)}, u32[]{:S(2)}) %all-to-all-start) | async-done | bytes 2359328 | tf_op jit(solution)/shard_map/all_to_all | solution.py:92
  405.0 3.4 reshape.354
  (95 shorter events, 39.1 us)
Async XLA Ops:
  0.0 69.8 %copy-start.17 = (s32[8,8,1]{1,2,0:T(1,128)S(1)}, s32[8,8,1]{1,2,0:T(1,128)}, u32[]{:S(2)}) copy-start(s32[8,8,1]{1,2,0:T(1,128)} %param.14) | copy-start | bytes 772
  0.0 54.3 %collective-permute-start = (bf16[2,1,1,1,1,384,1536]{6,5,3,2,0,4,1:T(8,128)(2,1)}, bf16[2,1,1,1,1,384,1536]{6,5,3,2,0,4,1:T(8,128)(2,1)S(1)}, u32[]{:S(2)}, u32[]{:S(2)}) collective-permute-start(bf16[2,1,1,1,1,384,1536]{6,5,3,2,0,4,1:T(8,128)(2,1)} %bitcast.214), channel_id=1, source_target_pairs={{0,8},{8,16},{16,24},{24,32},{32,40},{40,48},{48,56},{1,9},{9,17},... | collective-permute-start | bytes 7077896 | tf_op jit(solution)/shard_map/ppermute | solution.py:21
  3.3 53.9 %collective-permute-start.1 = (bf16[2,1,1,1,1,384,1536]{6,5,3,2,0,4,1:T(8,128)(2,1)}, bf16[2,1,1,1,1,384,1536]{6,5,3,2,0,4,1:T(8,128)(2,1)S(1)}, u32[]{:S(2)}, u32[]{:S(2)}) collective-permute-start(bf16[2,1,1,1,1,384,1536]{6,5,3,2,0,4,1:T(8,128)(2,1)} %bitcast.215), channel_id=1, source_target_pairs={{8,0},{16,8},{24,16},{32,24},{40,32},{48,40},{56,48},{9,1},{17,9},... | collective-permute-start | bytes 7077896 | tf_op jit(solution)/shard_map/ppermute | solution.py:22
  54.3 8.4 %copy-start.1 = (bf16[2,1,1,1,1,384,1536]{6,5,3,2,0,4,1:T(8,128)(2,1)}, bf16[2,1,1,1,1,384,1536]{6,5,3,2,0,4,1:T(8,128)(2,1)S(1)}, u32[]{:S(2)}) copy-start(bf16[2,1,1,1,1,384,1536]{6,5,3,2,0,4,1:T(8,128)(2,1)S(1)} %collective-permute-done) | copy-start | bytes 7077892
  57.2 5.6 %copy-start.3 = (bf16[2,1,1,1,1,384,1536]{6,5,3,2,0,4,1:T(8,128)(2,1)}, bf16[2,1,1,1,1,384,1536]{6,5,3,2,0,4,1:T(8,128)(2,1)S(1)}, u32[]{:S(2)}) copy-start(bf16[2,1,1,1,1,384,1536]{6,5,3,2,0,4,1:T(8,128)(2,1)S(1)} %collective-permute-done.1) | copy-start | bytes 7077892
  62.8 86.1 %copy-start = (bf16[2,1,1,1,1,384,1536]{6,5,4,3,2,1,0:T(8,128)(2,1)S(1)}, bf16[2,1,1,1,1,384,1536]{6,5,4,3,2,1,0:T(8,128)(2,1)}, u32[]{:S(2)}) copy-start(bf16[2,1,1,1,1,384,1536]{6,5,4,3,2,1,0:T(8,128)(2,1)} %param.9) | copy-start | bytes 7077892
  62.8 81.7 %collective-permute-start.2 = (bf16[2,1,3,1,1,384,1536]{6,5,3,2,0,4,1:T(8,128)(2,1)}, bf16[2,1,3,1,1,384,1536]{6,5,3,2,0,4,1:T(8,128)(2,1)}, u32[]{:S(2)}, u32[]{:S(2)}) collective-permute-start(bf16[2,1,3,1,1,384,1536]{6,5,3,2,0,4,1:T(8,128)(2,1)} %pad_maximum_fusion.1), channel_id=1, source_target_pairs={{0,1},{1,2},{2,3},{3,4},{4,5},{5,6},{6,7},{8,9},{9,10},{10,11},{11... | collective-permute-start | bytes 21233672 | tf_op jit(solution)/shard_map/ppermute | solution.py:21
  67.9 81.0 %collective-permute-start.3 = (bf16[2,1,3,1,1,384,1536]{6,5,3,2,0,4,1:T(8,128)(2,1)}, bf16[2,1,3,1,1,384,1536]{6,5,3,2,0,4,1:T(8,128)(2,1)}, u32[]{:S(2)}, u32[]{:S(2)}) collective-permute-start(bf16[2,1,3,1,1,384,1536]{6,5,3,2,0,4,1:T(8,128)(2,1)} %pad_maximum_fusion.1), channel_id=1, source_target_pairs={{1,0},{2,1},{3,2},{4,3},{5,4},{6,5},{7,6},{9,8},{10,9},{11,10},{12... | collective-permute-start | bytes 21233672 | tf_op jit(solution)/shard_map/ppermute | solution.py:22
  71.7 77.2 %copy-start.2 = (bf16[2,1,1,1,1,384,1536]{6,5,3,2,0,4,1:T(8,128)(2,1)S(1)}, bf16[2,1,1,1,1,384,1536]{6,5,3,2,0,4,1:T(8,128)(2,1)}, u32[]{:S(2)}) copy-start(bf16[2,1,1,1,1,384,1536]{6,5,3,2,0,4,1:T(8,128)(2,1)} %copy-done.1) | copy-start | bytes 7077892
  220.4 9.0 %copy-start.15 = (bf16[1,1,3456,256]{2,3,1,0:T(8,128)(2,1)S(1)}, bf16[1,1,3456,256]{2,3,1,0:T(8,128)(2,1)}, u32[]{:S(2)}) copy-start(bf16[1,1,3456,256]{2,3,1,0:T(8,128)(2,1)} %copy.117) | copy-start | bytes 5308420
  229.5 6.0 %copy-start.13 = (bf16[1,1,3456,256]{2,3,1,0:T(8,128)(2,1)S(1)}, bf16[1,1,3456,256]{2,3,1,0:T(8,128)(2,1)}, u32[]{:S(2)}) copy-start(bf16[1,1,3456,256]{2,3,1,0:T(8,128)(2,1)} %copy.144) | copy-start | bytes 5308420
  235.4 9.0 %copy-start.12 = (bf16[1,1,3456,256]{2,3,1,0:T(8,128)(2,1)S(1)}, bf16[1,1,3456,256]{2,3,1,0:T(8,128)(2,1)}, u32[]{:S(2)}) copy-start(bf16[1,1,3456,256]{2,3,1,0:T(8,128)(2,1)} %copy.139) | copy-start | bytes 5308420
  244.4 9.0 %copy-start.11 = (bf16[1,1,3456,256]{2,3,1,0:T(8,128)(2,1)S(1)}, bf16[1,1,3456,256]{2,3,1,0:T(8,128)(2,1)}, u32[]{:S(2)}) copy-start(bf16[1,1,3456,256]{2,3,1,0:T(8,128)(2,1)} %copy.134) | copy-start | bytes 5308420
  253.5 9.5 %copy-start.10 = (bf16[1,1,3456,256]{2,3,1,0:T(8,128)(2,1)S(1)}, bf16[1,1,3456,256]{2,3,1,0:T(8,128)(2,1)}, u32[]{:S(2)}) copy-start(bf16[1,1,3456,256]{2,3,1,0:T(8,128)(2,1)} %copy.129) | copy-start | bytes 5308420
  263.0 9.5 %copy-start.9 = (bf16[1,1,3456,256]{2,3,1,0:T(8,128)(2,1)S(1)}, bf16[1,1,3456,256]{2,3,1,0:T(8,128)(2,1)}, u32[]{:S(2)}) copy-start(bf16[1,1,3456,256]{2,3,1,0:T(8,128)(2,1)} %copy.124) | copy-start | bytes 5308420
  272.5 9.9 %copy-start.8 = (bf16[1,1,3456,256]{2,3,1,0:T(8,128)(2,1)S(1)}, bf16[1,1,3456,256]{2,3,1,0:T(8,128)(2,1)}, u32[]{:S(2)}) copy-start(bf16[1,1,3456,256]{2,3,1,0:T(8,128)(2,1)} %copy.123) | copy-start | bytes 5308420
  282.4 5.3 %copy-start.16 = (bf16[1,384,1536]{1,2,0:T(8,128)(2,1)S(1)}, bf16[1,384,1536]{1,2,0:T(8,128)(2,1)}, u32[]{:S(2)}) copy-start(bf16[1,384,1536]{1,2,0:T(8,128)(2,1)} %constant_dynamic-update-slice_fusion.5) | copy-start | bytes 3538948
  282.4 5.4 %copy-start.7 = (bf16[1,1,3456,256]{2,3,1,0:T(8,128)(2,1)S(1)}, bf16[1,1,3456,256]{2,3,1,0:T(8,128)(2,1)}, u32[]{:S(2)}) copy-start(bf16[1,1,3456,256]{2,3,1,0:T(8,128)(2,1)} %copy.128) | copy-start | bytes 5308420
  282.4 7.9 %copy-start.20 = (f32[2,384,3456]{1,2,0:T(8,128)S(1)}, f32[2,384,3456]{1,2,0:T(8,128)}, u32[]{:S(2)}) copy-start(f32[2,384,3456]{1,2,0:T(8,128)} %get-tuple-element.28) | copy-start | bytes 31850500
  282.4 7.9 %copy-start.22 = (f32[2,384]{1,0:T(2,128)S(1)}, f32[2,384]{1,0:T(2,128)}, u32[]{:S(2)}) copy-start(f32[2,384]{1,0:T(2,128)} %get-tuple-element.27) | copy-start | bytes 9220
  282.4 9.1 %slice-start.6 = ((s8[10616832]{0:T(1024)(128)(4,1)}), s8[4194304]{0:T(1024)(128)(4,1)S(1)}, s32[]{:S(2)}) async-start(s8[10616832]{0:T(1024)(128)(4,1)} %bitcast.249), calls=%async_computation.7 | async-start | bytes 8388608
  282.4 10.3 %slice-start.7 = ((s8[10616832]{0:T(1024)(128)(4,1)}), s8[4194304]{0:T(1024)(128)(4,1)S(1)}, s32[]{:S(2)}) async-start(s8[10616832]{0:T(1024)(128)(4,1)} %bitcast.249), calls=%async_computation.8 | async-start | bytes 8388608
  290.4 3.7 slice-start.8
  290.4 3.7 copy-start.21
  294.1 7.4 %slice-start.3 = ((s8[10616832]{0:T(1024)(128)(4,1)}), s8[4194304]{0:T(1024)(128)(4,1)S(1)}, s32[]{:S(2)}) async-start(s8[10616832]{0:T(1024)(128)(4,1)} %bitcast.247), calls=%async_computation.4 | async-start | bytes 8388608
  294.1 7.4 %slice-start.4 = ((s8[10616832]{0:T(1024)(128)(4,1)}), s8[4194304]{0:T(1024)(128)(4,1)S(1)}, s32[]{:S(2)}) async-start(s8[10616832]{0:T(1024)(128)(4,1)} %bitcast.247), calls=%async_computation.5 | async-start | bytes 8388608
  295.6 6.2 %copy-start.4 = (bf16[1,1,3456,256]{2,3,1,0:T(8,128)(2,1)S(1)}, bf16[1,1,3456,256]{2,3,1,0:T(8,128)(2,1)}, u32[]{:S(2)}) copy-start(bf16[1,1,3456,256]{2,3,1,0:T(8,128)(2,1)} %copy.143) | copy-start | bytes 5308420
  295.6 6.9 %slice-start.5 = ((s8[10616832]{0:T(1024)(128)(4,1)}), s8[2228224]{0:T(1024)(128)(4,1)S(1)}, s32[]{:S(2)}) async-start(s8[10616832]{0:T(1024)(128)(4,1)} %bitcast.247), calls=%async_computation.6 | async-start | bytes 4456448
  295.6 8.1 %slice-start = ((s8[9437184]{0:T(1024)(128)(4,1)}), s8[4194304]{0:T(1024)(128)(4,1)S(1)}, s32[]{:S(2)}) async-start(s8[9437184]{0:T(1024)(128)(4,1)} %bitcast.244), calls=%async_computation.1 | async-start | bytes 8388608
  295.6 9.2 %slice-start.1 = ((s8[9437184]{0:T(1024)(128)(4,1)}), s8[4194304]{0:T(1024)(128)(4,1)S(1)}, s32[]{:S(2)}) async-start(s8[9437184]{0:T(1024)(128)(4,1)} %bitcast.244), calls=%async_computation.2 | async-start | bytes 8388608
  302.5 3.4 copy-start.19
  371.3 33.7 %all-to-all-start = ((bf16[2,2,294912]{2,1,0:T(2,128)(2,1)}), bf16[2,2,294912]{2,1,0:T(2,128)(2,1)S(1)}, u32[]{:S(2)}, u32[]{:S(2)}) async-start(bf16[2,2,294912]{2,1,0:T(2,128)(2,1)} %reshape.353), calls=%async_computation | async-start | bytes 4718592 | tf_op jit(solution)/shard_map/all_to_all | solution.py:92
  (5 other events, 12.9 us)
where the time goes:
time: 421 us; the launch traced here: 413 us
  waiting for transfers between devices  155 us (37%)
  local copies, waits for them, and re-layouts  88.3 us (21%)
  matrix products  80.1 us (19%)
  other arithmetic  71.7 us (17%)
  starting transfers between devices  17.4 us (4%)
    ppermute x2, waiting for transfers between devices, with_halo(): before = lax.ppermute(last, axis, up)  119 us
    sub x6, matrix products, attend_group(): exponent = jnp.exp(scores - row_max)  55.9 us
    unnamed x4, other arithmetic  50.8 us
    slice x7, local copies, waits for them, and re-layouts, on_device(): key_part = windows[0, :, :, start_col:stop_col]  35.6 us
    all_to_all x1, waiting for transfers between devices, on_device(): lax.all_to_all(prediction, 'cfg', split_axis=5, concat_axis=0, tiled=True)  28.2 us
    slice x6, local copies, waits for them, and re-layouts, on_device(): value_part = windows[1, :, :, start_col:stop_col]  21.9 us
    dot_general x6, matrix products, attend_group(): jnp.einsum('whqk,wkhd->wqhd', probs, value_rows, preferred_element_type=j...  19.8 us
    concatenate x2, other arithmetic, with_halo(): shard = jnp.concatenate([before, shard, after], axis=dim)  19.7 us
  transfers between devices with their start and end apart: 5, of which 5 were waited for; matrix products, arithmetic and copies ran while one was open for 1% of the time, Pallas kernels for 0%

commit v1 on v0

v1 whole, which is shorter than its diff:
```python
import functools
import math

import jax
import jax.numpy as jnp
from jax import lax
from jax.experimental import pallas as pl
from jax.experimental.pallas import tpu as pltpu
from jax.sharding import PartitionSpec as P

HEAD_DIM = 128
GROUP = 2
DEPTH = 2
CHUNKS = 4
MASKED = -1e30
MESH = pl.DeviceIdType.MESH


def kernel(
    query, keyval, hidden, weight, gate, guidance, counts, out,
    q_buf, kv_buf, w_buf, hid_buf, o_own, o_out, o_in, l_own, l_out, l_in,
    acc, pred_out, pred_in, result,
    kv_send, kv_recv, q_send, q_recv, o_send, o_recv, l_send, l_recv,
    p_send, p_recv, kv_sem, q_sem, w_sem, hid_sem, out_sem,
):
    rows, channels = query.shape[4], query.shape[5]
    width = GROUP * HEAD_DIM
    groups = channels // width
    model = hidden.shape[5]
    half = model // 2
    scale = HEAD_DIM**-0.5 * math.log2(math.e)

    c, t, h = lax.axis_index("cfg"), lax.axis_index("tm"), lax.axis_index("height")
    times, heights = lax.axis_size("tm"), lax.axis_size("height")
    has_left, has_right = t > 0, t < times - 1
    has_up, has_down = h > 0, h < heights - 1
    left, right, up, down = {"tm": t - 1}, {"tm": t + 1}, {"height": h - 1}, {"height": h + 1}
    other = {"cfg": 1 - c}

    def cols(g):
        return pl.ds(pl.multiple_of(g * width, width), width)

    def kv_local(g):
        return pltpu.make_async_copy(
            keyval.at[:, 0, 0, 0, 0, :, cols(g)], kv_buf.at[1, g], kv_sem.at[g]
        )

    def q_local(g):
        return pltpu.make_async_copy(
            query.at[0, 0, 0, 0, :, cols(g)], q_buf.at[1, g], q_sem.at[g]
        )

    def kv_copy(side, g):
        return pltpu.make_async_remote_copy(
            keyval.at[:, 0, 0, 0, 0, :, cols(g)],
            kv_buf.at[2 - 2 * side, g],
            kv_send.at[side, g],
            kv_recv.at[1 - side, g],
            device_id=(left, right)[side],
            device_id_type=MESH,
        )

    def q_copy(side, g):
        return pltpu.make_async_remote_copy(
            query.at[0, 0, 0, 0, :, cols(g)],
            q_buf.at[2 - 2 * side, g],
            q_send.at[side, g],
            q_recv.at[1 - side, g],
            device_id=(up, down)[side],
            device_id_type=MESH,
        )

    def o_copy(side, g):
        return pltpu.make_async_remote_copy(
            o_out.at[side, g],
            o_in.at[1 - side, g],
            o_send.at[side, g],
            o_recv.at[1 - side, g],
            device_id=(up, down)[side],
            device_id_type=MESH,
        )

    def l_copy(side, g):
        return pltpu.make_async_remote_copy(
            l_out.at[side, g],
            l_in.at[1 - side, g],
            l_send.at[side, g],
            l_recv.at[1 - side, g],
            device_id=(up, down)[side],
            device_id_type=MESH,
        )

    chunk = rows // CHUNKS

    def p_copy(k):
        piece = pl.ds(pl.multiple_of(k * chunk, chunk), chunk)
        return pltpu.make_async_remote_copy(
            pred_out.at[piece],
            pred_in.at[piece],
            p_send.at[k],
            p_recv.at[k],
            device_id=other,
            device_id_type=MESH,
        )

    has_tm, has_height = (has_left, has_right), (has_up, has_down)

    w_copy = pltpu.make_async_copy(weight, w_buf, w_sem)
    hid_copy = pltpu.make_async_copy(hidden.at[0, 0, 0, 0], hid_buf, hid_sem)
    for g in range(groups):
        kv_local(g).start()
        q_local(g).start()

    barrier = pltpu.get_barrier_semaphore()
    near = jnp.int32(1)
    pl.semaphore_signal(barrier, inc=1, device_id=other, device_id_type=MESH)
    for present, device in (
        (has_left, left), (has_right, right), (has_up, up), (has_down, down)
    ):
        near = near + present.astype(jnp.int32)

        @pl.when(present)
        def _():
            pl.semaphore_signal(barrier, inc=1, device_id=device, device_id_type=MESH)

    pl.semaphore_wait(barrier, near)

    for g in range(DEPTH):
        for side in range(2):
            pl.when(has_height[side])(q_copy(side, g).start)
            pl.when(has_tm[side])(kv_copy(side, g).start)
    w_copy.start()
    hid_copy.start()

    for side in range(2):

        @pl.when(jnp.logical_not(has_tm[side]))
        def _():
            kv_buf[2 * side] = jnp.zeros(kv_buf.shape[1:], kv_buf.dtype)

        @pl.when(jnp.logical_not(has_height[side]))
        def _():
            o_in[side] = jnp.zeros(o_in.shape[1:], o_in.dtype)
            l_in[side] = jnp.full(l_in.shape[1:], MASKED, l_in.dtype)

    position = lax.broadcasted_iota(jnp.int32, (1, rows), 1)
    live = []
    for step in (-1, 0, 1):
        at = jnp.clip(t + step, 0, times - 1)
        inside = (t + step >= 0) & (t + step < times)
        live.append(position < jnp.where(inside, counts[at, h, 0], 0))
    own_count = counts[t, h, 0]
    query_live = (
        lax.broadcasted_iota(jnp.int32, (rows, HEAD_DIM), 0) < own_count
    ).astype(jnp.float32)
    low_lanes = lax.broadcasted_iota(jnp.int32, (rows, HEAD_DIM), 1) < HEAD_DIM // 2
    ones = jnp.ones((rows, HEAD_DIM), jnp.bfloat16)

    def attend_head(tile, g, j):
        at = slice(j * HEAD_DIM, (j + 1) * HEAD_DIM)
        q = q_buf[tile, g, :, at]
        scores = []
        for i in range(3):
            s = lax.dot_general(
                q, kv_buf[i, g, 0, :, at], (((1,), (1,)), ((), ())),
                preferred_element_type=jnp.float32,
            )
            scores.append(jnp.where(live[i], s, MASKED))
        top = jnp.maximum(jnp.maximum(scores[0], scores[1]), scores[2])
        top = jnp.max(top, axis=1, keepdims=True)
        mixed = jnp.zeros((rows, 2 * HEAD_DIM), jnp.float32)
        for i in range(3):
            p = jnp.exp2((scores[i] - top) * scale).astype(jnp.bfloat16)
            v = jnp.concatenate([kv_buf[i, g, 1, :, at], ones], axis=1)
            mixed = mixed + jnp.dot(p, v, preferred_element_type=jnp.float32)
        total = mixed[:, HEAD_DIM:]
        result = mixed[:, :HEAD_DIM] / total
        return result, top * scale + jnp.log(total) * math.log2(math.e)

    def attend(g):
        def one(tile):
            heads = [attend_head(tile, g, j) for j in range(GROUP)]
            mixed = jnp.concatenate([x for x, _ in heads], axis=1)
            return mixed, jnp.where(low_lanes, heads[0][1], heads[1][1])

        for side in range(2):

            @pl.when(has_height[side])
            def _():
                q_copy(1 - side, g).wait_recv()
                mixed, level = one(2 * side)
                o_out[side, g] = mixed.astype(jnp.bfloat16)
                l_out[side, g] = level
                o_copy(side, g).start()
                l_copy(side, g).start()

        mixed, level = one(1)
        o_own[g] = mixed
        l_own[g] = level

    def combine(g):
        for side in range(2):

            @pl.when(has_height[side])
            def _():
                o_copy(1 - side, g).wait_recv()
                l_copy(1 - side, g).wait_recv()

        levels = [l_in[0, g], l_own[g], l_in[1, g]]
        top = jnp.maximum(jnp.maximum(levels[0], levels[1]), levels[2])
        shares = [jnp.exp2(x - top) for x in levels]
        total = shares[0] + shares[1] + shares[2]
        shares = [x / total * query_live for x in shares]
        parts = []
        for j in range(GROUP):
            at = slice(j * HEAD_DIM, (j + 1) * HEAD_DIM)
            lane = j * HEAD_DIM // 2
            parts.append(
                shares[0][:, lane : lane + 1] * o_in[0, g, :, at].astype(jnp.float32)
                + shares[1][:, lane : lane + 1] * o_own[g, :, at]
                + shares[2][:, lane : lane + 1] * o_in[1, g, :, at].astype(jnp.float32)
            )
        attended = jnp.concatenate(parts, axis=1).astype(jnp.bfloat16)
        block = 512
        depth = pl.ds(pl.multiple_of(g * width, width), width)

        def add(k, carry):
            at = pl.ds(pl.multiple_of(k * block, block), block)
            acc[:, at] += jnp.dot(
                attended, w_buf[depth, at], preferred_element_type=jnp.float32
            )
            return carry

        lax.fori_loop(0, model // block, add, 0)

    acc[...] = jnp.zeros_like(acc)
    w_copy.wait()

    def step(g, carry):
        for side in range(2):

            @pl.when(has_tm[side])
            def _():
                kv_copy(1 - side, g).wait_recv()

        kv_local(g).wait()
        q_local(g).wait()

        @pl.when(g + DEPTH < groups)
        def _():
            for side in range(2):
                pl.when(has_height[side])(q_copy(side, g + DEPTH).start)
                pl.when(has_tm[side])(kv_copy(side, g + DEPTH).start)

        attend(g)

        @pl.when(g > 0)
        def _():
            combine(g - 1)

        return carry

    lax.fori_loop(0, groups, step, 0)
    combine(groups - 1)
    hid_copy.wait()

    def predict(k, side):
        piece = pl.ds(pl.multiple_of(k * chunk, chunk), chunk)
        at = pl.ds(pl.multiple_of(side * half, half), half)
        stream = hid_buf[piece, at].astype(jnp.float32)
        return (stream + gate[:, at] * acc[piece, at]).astype(jnp.bfloat16)

    for k in range(CHUNKS):
        pred_out[k * chunk : (k + 1) * chunk] = predict(k, 1 - c)
        p_copy(k).start()
    for k in range(CHUNKS):
        piece = slice(k * chunk, (k + 1) * chunk)
        mine = predict(k, c).astype(jnp.float32)
        p_copy(k).wait_recv()
        theirs = pred_in[piece].astype(jnp.float32)
        cond = jnp.where(c == 0, mine, theirs)
        uncond = jnp.where(c == 0, theirs, mine)
        result[piece] = (uncond + guidance[0] * (cond - uncond)).astype(jnp.bfloat16)
        pltpu.make_async_copy(result.at[piece], out.at[0, 0, 0, piece], out_sem.at[k]).start()
    for k in range(CHUNKS):
        piece = slice(k * chunk, (k + 1) * chunk)
        pltpu.make_async_copy(result.at[piece], out.at[0, 0, 0, piece], out_sem.at[k]).wait()
        p_copy(k).wait_send()

    def drain(g, carry):
        for side in range(2):

            @pl.when(has_tm[side])
            def _():
                kv_copy(side, g).wait_send()

            @pl.when(has_height[side])
            def _():
                q_copy(side, g).wait_send()
                o_copy(side, g).wait_send()
                l_copy(side, g).wait_send()

        return carry

    lax.fori_loop(0, groups, drain, 0)


def on_device(query, keyval, hidden, out_weight, gate_scale, guidance, counts):
    rows, channels = query.shape[4], query.shape[5]
    model = hidden.shape[5]
    width = GROUP * HEAD_DIM
    groups = channels // width
    bf16, f32, dma = jnp.bfloat16, jnp.float32, pltpu.SemaphoreType.DMA
    anywhere = pl.BlockSpec(memory_space=pl.ANY)
    vmem = pl.BlockSpec(memory_space=pltpu.VMEM)
    smem = pl.BlockSpec(memory_space=pltpu.SMEM)
    return pl.pallas_call(
        kernel,
        out_shape=jax.ShapeDtypeStruct((1, 1, 1, rows, model // 2), bf16),
        in_specs=[anywhere, anywhere, anywhere, anywhere, vmem, smem, smem],
        out_specs=anywhere,
        scratch_shapes=[
            pltpu.VMEM((3, groups, rows, width), bf16),
            pltpu.VMEM((3, groups, 2, rows, width), bf16),
            pltpu.VMEM((channels, model), bf16),
            pltpu.VMEM((rows, model), bf16),
            pltpu.VMEM((groups, rows, width), f32),
            pltpu.VMEM((2, groups, rows, width), bf16),
            pltpu.VMEM((2, groups, rows, width), bf16),
            pltpu.VMEM((groups, rows, HEAD_DIM), f32),
            pltpu.VMEM((2, groups, rows, HEAD_DIM), f32),
            pltpu.VMEM((2, groups, rows, HEAD_DIM), f32),
            pltpu.VMEM((rows, model), f32),
            pltpu.VMEM((rows, model // 2), bf16),
            pltpu.VMEM((rows, model // 2), bf16),
            pltpu.VMEM((rows, model // 2), bf16),
        ]
        + [dma((2, groups))] * 8
        + [dma((CHUNKS,))] * 2
        + [dma((groups,))] * 2
        + [dma, dma, dma((CHUNKS,))],
        compiler_params=pltpu.CompilerParams(
            collective_id=0, has_side_effects=True, vmem_limit_bytes=60 * 2**20
        ),
    )(query, keyval, hidden, out_weight, gate_scale, guidance, counts)


def solution(mesh):
    return jax.shard_map(
        on_device,
        mesh=mesh,
        in_specs=(
            P("cfg", "tm", "height", None, None, None),
            P(None, "cfg", "tm", "height", None, None, None),
            P("cfg", "tm", "height", None, None, None),
            P(),
            P("cfg", None),
            P(),
            P(),
        ),
        out_specs=P("tm", "height", None, None, "cfg"),
        check_vma=False,
    )
```

time: 421 us -> 105 us (0.25); the launches traced: 413 us -> 103 us
  waiting for transfers between devices: 155 us -> 0 us
  Pallas kernels: 0 us -> 98.8 us
  local copies, waits for them, and re-layouts: 88.3 us -> 3.78 us
  matrix products: 80.1 us -> 0 us
  other arithmetic: 71.7 us -> 0 us
  starting transfers between devices: 17.4 us -> 0 us
    ppermute x4 -> x0, waiting for transfers between devices: 126 us -> none  [the longest x2 119 us: with_halo(): before = lax.ppermute(last, axis, up)]
    pallas_call x0 -> x1, Pallas kernels: none -> 98.8 us  [on_device(): pl.pallas_call(kernel, out_shape=jax.ShapeDtypeStruct((1, 1, 1, rows, mod...]
    slice x16 -> x0, local copies, waits for them, and re-layouts: 59.2 us -> none  [the longest x7 35.6 us: on_device(): key_part = windows[0, :, :, start_col:stop_col]]
    sub x6 -> x0, matrix products: 55.9 us -> none  [attend_group(): exponent = jnp.exp(scores - row_max)]
    unnamed x4 -> x0, other arithmetic: 50.8 us -> none
    all_to_all x1 -> x0, waiting for transfers between devices: 28.2 us -> none  [on_device(): lax.all_to_all(prediction, 'cfg', split_axis=5, concat_axis=0, tiled=True)]
    dot_general x7 -> x0, matrix products: 24.1 us -> none  [the longest x6 19.8 us: attend_group(): jnp.einsum('whqk,wkhd->wqhd', probs, value_rows, preferred_element_type=j...]
    concatenate x2 -> x0, other arithmetic: 19.7 us -> none  [with_halo(): shard = jnp.concatenate([before, shard, after], axis=dim)]
  transfers between devices with their start and end apart: 5 -> 0, of which waited for: 5 -> 0; matrix products, arithmetic and copies ran while one was open for 1% -> 0% of each run, Pallas kernels for 0% -> 0%
where the time goes in v1:
time: 105 us; the launch traced here: 103 us
  Pallas kernels  98.8 us (94%)
  local copies, waits for them, and re-layouts  3.78 us (4%)
    pallas_call x1, Pallas kernels, on_device(): pl.pallas_call(kernel, out_shape=jax.ShapeDtypeStruct((1, 1, 1, rows, mod...  98.8 us
    unnamed x2, local copies, waits for them, and re-layouts  3.78 us

profile of v1, /device:TPU:11, one launch (start us, length us, event | category | flops | bytes accessed | tf_op | source)
XLA Modules:
  0.0 103.2 jit_solution(8503090349545441367)
XLA Ops:
  0.7 1.4 %copy.8.counts = s32[8,8,1]{2,1,0:T(8,128)} copy(s32[8,8,1]{1,2,0:T(1,128)} %param.13) | data formatting | bytes 512 | tf_op args[6]
  2.1 98.8 %shard_map.73 = bf16[1,1,1,384,1536]{4,3,2,1,0:T(8,128)(2,1)} custom-call(bf16[1,1,1,1,384,1536]{5,4,3,2,1,0:T(8,128)(2,1)} %query.1, bf16[2,1,1,1,1,384,1536]{6,5,4,3,2,1,0:T(8,128)(2,1)} %keyval.1, bf16[1,1,1,1,384,3072]{5,4,3,2,1,0:T(8,128)(2,1)} %hidden.1, bf16[1536,3072]{1,0:T(8,128)(2,1)} %weight.1, f32[1,3072]{1,0:T(1,128)} %gate.1, ...), custom_call_target="tpu_custom_call" | custom-call | tf_op jit(solution)/shard_map/pallas_call | solution.py:317
  100.9 2.4 %copy.11 = bf16[1,1,1,384,1536]{4,3,2,1,0:T(8,128)(2,1)} copy(bf16[1,1,1,384,1536]{4,3,2,1,0:T(8,128)(2,1)} %shard_map.73) | data formatting | bytes 2359296

commit v2 on v1

--- a/solution.py
+++ b/solution.py
@@ -10,8 +10,9 @@
 
 HEAD_DIM = 128
 GROUP = 2
-DEPTH = 2
-CHUNKS = 4
+DEPTH = 4
+EARLY = 288
+CHUNKS = 2
 MASKED = -1e30
 MESH = pl.DeviceIdType.MESH
 
@@ -19,9 +20,9 @@
 def kernel(
     query, keyval, hidden, weight, gate, guidance, counts, out,
     q_buf, kv_buf, w_buf, hid_buf, o_own, o_out, o_in, l_own, l_out, l_in,
-    acc, pred_out, pred_in, result,
+    acc, acc_late, acc_in, pred_out, pred_in, a_out, a_in, hid_in, gate_in, result,
     kv_send, kv_recv, q_send, q_recv, o_send, o_recv, l_send, l_recv,
-    p_send, p_recv, kv_sem, q_sem, w_sem, hid_sem, out_sem,
+    a_send, a_recv, p_send, p_recv, x_send, x_recv, kv_sem, q_sem, w_sem, hid_sem, out_sem,
 ):
     rows, channels = query.shape[4], query.shape[5]
     width = GROUP * HEAD_DIM
@@ -50,13 +51,39 @@
             query.at[0, 0, 0, 0, :, cols(g)], q_buf.at[1, g], q_sem.at[g]
         )
 
+    middle = times // 2
+
+    def relayed(g):
+        return (g == 1) | (g == 2) | (g == 3)
+
     def kv_copy(side, g):
+        by = relayed(g) & (t == (middle, middle - 1)[side])
         return pltpu.make_async_remote_copy(
             keyval.at[:, 0, 0, 0, 0, :, cols(g)],
+            kv_buf.at[jnp.where(by, 2 * side, 2 - 2 * side), g],
+            kv_send.at[side, g],
+            kv_recv.at[jnp.where(by, side, 1 - side), g],
+            device_id={"tm": jnp.where(by, (0, times - 1)[side], t + (-1, 1)[side])},
+            device_id_type=MESH,
+        )
+
+    def kv_forward(side, g):
+        return pltpu.make_async_remote_copy(
+            kv_buf.at[2 * side, g],
             kv_buf.at[2 - 2 * side, g],
             kv_send.at[side, g],
             kv_recv.at[1 - side, g],
-            device_id=(left, right)[side],
+            device_id={"tm": (middle - 1, middle)[side]},
+            device_id_type=MESH,
+        )
+
+    def kv_arrival(side, g):
+        return pltpu.make_async_remote_copy(
+            kv_buf.at[2 * side, g],
+            kv_buf.at[2 * side, g],
+            kv_send.at[side, g],
+            kv_recv.at[side, g],
+            device_id=other,
             device_id_type=MESH,
         )
 
@@ -90,10 +117,21 @@
             device_id_type=MESH,
         )
 
-    chunk = rows // CHUNKS
+    def a_copy(g):
+        return pltpu.make_async_remote_copy(
+            a_out.at[:, cols(g)],
+            a_in.at[:, cols(g)],
+            a_send.at[g],
+            a_recv.at[g],
+            device_id=other,
+            device_id_type=MESH,
+        )
+
+    late = rows - EARLY
+    chunk = late // CHUNKS
 
     def p_copy(k):
-        piece = pl.ds(pl.multiple_of(k * chunk, chunk), chunk)
+        piece = pl.ds(k * chunk, chunk)
         return pltpu.make_async_remote_copy(
             pred_out.at[piece],
             pred_in.at[piece],
@@ -102,6 +140,20 @@
             device_id=other,
             device_id_type=MESH,
         )
+
+    mine = pl.ds(pl.multiple_of(c * half, half), half)
+    theirs = pl.ds(pl.multiple_of((1 - c) * half, half), half)
+    hid_swap = pltpu.make_async_remote_copy(
+        hidden.at[0, 0, 0, 0, :EARLY, theirs],
+        hid_in,
+        x_send.at[0],
+        x_recv.at[0],
+        device_id=other,
+        device_id_type=MESH,
+    )
+    gate_swap = pltpu.make_async_remote_copy(
+        gate, gate_in, x_send.at[1], x_recv.at[1], device_id=other, device_id_type=MESH
+    )
 
     has_tm, has_height = (has_left, has_right), (has_up, has_down)
 
@@ -123,6 +175,17 @@
         def _():
             pl.semaphore_signal(barrier, inc=1, device_id=device, device_id_type=MESH)
 
+    for at, far in (
+        (0, middle - 1), (0, middle), (middle - 1, 0),
+        (middle, 0), (times - 1, middle - 1), (times - 1, middle),
+        (middle - 1, times - 1), (middle, times - 1),
+    ):
+        near = near + (t == at).astype(jnp.int32)
+
+        @pl.when(t == at)
+        def _():
+            pl.semaphore_signal(barrier, inc=1, device_id={"tm": far}, device_id_type=MESH)
+
     pl.semaphore_wait(barrier, near)
 
     for g in range(DEPTH):
@@ -130,13 +193,17 @@
             pl.when(has_height[side])(q_copy(side, g).start)
             pl.when(has_tm[side])(kv_copy(side, g).start)
     w_copy.start()
+    hid_swap.start()
+    gate_swap.start()
     hid_copy.start()
 
     for side in range(2):
 
         @pl.when(jnp.logical_not(has_tm[side]))
         def _():
-            kv_buf[2 * side] = jnp.zeros(kv_buf.shape[1:], kv_buf.dtype)
+            for g in range(groups):
+                if not relayed(g):
+                    kv_buf[2 * side, g] = jnp.zeros(kv_buf.shape[2:], kv_buf.dtype)
 
         @pl.when(jnp.logical_not(has_height[side]))
         def _():
@@ -221,27 +288,38 @@
                 + shares[2][:, lane : lane + 1] * o_in[1, g, :, at].astype(jnp.float32)
             )
         attended = jnp.concatenate(parts, axis=1).astype(jnp.bfloat16)
+        a_out[:, cols(g)] = attended[:EARLY]
+        a_copy(g).start()
+        project(g, attended[EARLY:], acc_late, (1 - c) * half)
+        project(g, attended, acc, c * half)
+
+    def project(g, attended, total, first):
         block = 512
         depth = pl.ds(pl.multiple_of(g * width, width), width)
 
         def add(k, carry):
             at = pl.ds(pl.multiple_of(k * block, block), block)
-            acc[:, at] += jnp.dot(
-                attended, w_buf[depth, at], preferred_element_type=jnp.float32
+            column = pl.ds(pl.multiple_of(first + k * block, block), block)
+            total[:, at] += jnp.dot(
+                attended, w_buf[depth, column], preferred_element_type=jnp.float32
             )
             return carry
 
-        lax.fori_loop(0, model // block, add, 0)
-
+        lax.fori_loop(0, half // block, add, 0)
+
+    acc_late[...] = jnp.zeros_like(acc_late)
     acc[...] = jnp.zeros_like(acc)
     w_copy.wait()
 
     def step(g, carry):
         for side in range(2):
-
-            @pl.when(has_tm[side])
+            end = t == (0, times - 1)[side]
+            pl.when(has_tm[side])(kv_arrival(side, g).wait_recv)
+
+            @pl.when(end & relayed(g + 1))
             def _():
-                kv_copy(1 - side, g).wait_recv()
+                kv_arrival(side, g + 1).wait_recv()
+                kv_forward(side, g + 1).start()
 
         kv_local(g).wait()
         q_local(g).wait()
@@ -263,36 +341,63 @@
     lax.fori_loop(0, groups, step, 0)
     combine(groups - 1)
     hid_copy.wait()
-
-    def predict(k, side):
-        piece = pl.ds(pl.multiple_of(k * chunk, chunk), chunk)
-        at = pl.ds(pl.multiple_of(side * half, half), half)
-        stream = hid_buf[piece, at].astype(jnp.float32)
-        return (stream + gate[:, at] * acc[piece, at]).astype(jnp.bfloat16)
-
-    for k in range(CHUNKS):
-        pred_out[k * chunk : (k + 1) * chunk] = predict(k, 1 - c)
-        p_copy(k).start()
     for k in range(CHUNKS):
         piece = slice(k * chunk, (k + 1) * chunk)
-        mine = predict(k, c).astype(jnp.float32)
+        stream = hid_buf[EARLY + k * chunk : EARLY + (k + 1) * chunk, theirs]
+        pred_out[piece] = (
+            stream.astype(jnp.float32) + gate[:, theirs] * acc_late[piece]
+        ).astype(jnp.bfloat16)
+        p_copy(k).start()
+    for g in range(groups):
+        a_copy(g).wait_recv()
+
+    def project_in(k, carry):
+        at = pl.ds(pl.multiple_of(k * 256, 256), 256)
+        column = pl.ds(pl.multiple_of(c * half + k * 256, 256), 256)
+        acc_in[:, at] = jnp.dot(
+            a_in[...], w_buf[:, column], preferred_element_type=jnp.float32
+        )
+        return carry
+
+    lax.fori_loop(0, half // 256, project_in, 0)
+    hid_swap.wait_recv()
+    gate_swap.wait_recv()
+
+    def guide(k, size, their_pred):
+        piece = pl.ds(k * size, size)
+        stream = hid_buf[piece, mine].astype(jnp.float32)
+        own = (stream + gate[:, mine] * acc[piece]).astype(jnp.bfloat16).astype(jnp.float32)
+        cond = jnp.where(c == 0, own, their_pred)
+        uncond = jnp.where(c == 0, their_pred, own)
+        result[piece] = (uncond + guidance[0] * (cond - uncond)).astype(jnp.bfloat16)
+
+    def store(k):
+        piece = pl.ds(k * chunk, chunk)
+        return pltpu.make_async_copy(result.at[piece], out.at[0, 0, 0, piece], out_sem.at[k])
+
+    before = EARLY // chunk
+    for k in range(before):
+        piece = slice(k * chunk, (k + 1) * chunk)
+        pred = hid_in[piece].astype(jnp.float32) + gate_in[:, mine] * acc_in[piece]
+        guide(k, chunk, pred.astype(jnp.bfloat16).astype(jnp.float32))
+        store(k).start()
+    for k in range(CHUNKS):
         p_copy(k).wait_recv()
-        theirs = pred_in[piece].astype(jnp.float32)
-        cond = jnp.where(c == 0, mine, theirs)
-        uncond = jnp.where(c == 0, theirs, mine)
-        result[piece] = (uncond + guidance[0] * (cond - uncond)).astype(jnp.bfloat16)
-        pltpu.make_async_copy(result.at[piece], out.at[0, 0, 0, piece], out_sem.at[k]).start()
+        guide(before + k, chunk, pred_in[k * chunk : (k + 1) * chunk].astype(jnp.float32))
+        store(before + k).start()
+    for k in range(before + CHUNKS):
+        store(k).wait()
     for k in range(CHUNKS):
-        piece = slice(k * chunk, (k + 1) * chunk)
-        pltpu.make_async_copy(result.at[piece], out.at[0, 0, 0, piece], out_sem.at[k]).wait()
         p_copy(k).wait_send()
+    hid_swap.wait_send()
+    gate_swap.wait_send()
 
     def drain(g, carry):
+        a_copy(g).wait_send()
         for side in range(2):
-
-            @pl.when(has_tm[side])
-            def _():
-                kv_copy(side, g).wait_send()
+            end = t == (0, times - 1)[side]
+            pl.when(has_tm[side])(kv_copy(side, g).wait_send)
+            pl.when(end & relayed(g))(kv_forward(side, g).wait_send)
 
             @pl.when(has_height[side])
             def _():
@@ -330,15 +435,23 @@
             pltpu.VMEM((groups, rows, HEAD_DIM), f32),
             pltpu.VMEM((2, groups, rows, HEAD_DIM), f32),
             pltpu.VMEM((2, groups, rows, HEAD_DIM), f32),
-            pltpu.VMEM((rows, model), f32),
-            pltpu.VMEM((rows, model // 2), bf16),
-            pltpu.VMEM((rows, model // 2), bf16),
+            pltpu.VMEM((rows, model // 2), f32),
+            pltpu.VMEM((rows - EARLY, model // 2), f32),
+            pltpu.VMEM((EARLY, model // 2), f32),
+            pltpu.VMEM((rows - EARLY, model // 2), bf16),
+            pltpu.VMEM((rows - EARLY, model // 2), bf16),
+            pltpu.VMEM((EARLY, channels), bf16),
+            pltpu.VMEM((EARLY, channels), bf16),
+            pltpu.VMEM((EARLY, model // 2), bf16),
+            pltpu.VMEM((1, model), f32),
             pltpu.VMEM((rows, model // 2), bf16),
         ]
         + [dma((2, groups))] * 8
+        + [dma((groups,))] * 2
         + [dma((CHUNKS,))] * 2
+        + [dma((2,))] * 2
         + [dma((groups,))] * 2
-        + [dma, dma, dma((CHUNKS,))],
+        + [dma, dma, dma((rows * CHUNKS // (rows - EARLY),))],
         compiler_params=pltpu.CompilerParams(
             collective_id=0, has_side_effects=True, vmem_limit_bytes=60 * 2**20
         ),

time: 105 us -> 86.6 us (0.82)
  Pallas kernels: 98.8 us -> 81.4 us
    pallas_call x1, Pallas kernels: 98.8 us -> 81.4 us  [on_device(): pl.pallas_call(kernel, out_shape=jax.ShapeDtypeStruct((1, 1, 1, rows, mod...]
where the time goes in v2:
time: 86.6 us; the launch traced here: 85.8 us
  Pallas kernels  81.4 us (94%)
  local copies, waits for them, and re-layouts  3.78 us (4%)
    pallas_call x1, Pallas kernels, on_device(): pl.pallas_call(kernel, out_shape=jax.ShapeDtypeStruct((1, 1, 1, rows, mod...  81.4 us
    unnamed x2, local copies, waits for them, and re-layouts  3.78 us

profile of v2, /device:TPU:11, one launch (start us, length us, event | category | flops | bytes accessed | tf_op | source)
XLA Modules:
  0.0 85.8 jit_solution(5335074822267306397)
XLA Ops:
  0.7 1.4 %copy.8.counts = s32[8,8,1]{2,1,0:T(8,128)} copy(s32[8,8,1]{1,2,0:T(1,128)} %param.13) | data formatting | bytes 512 | tf_op args[6]
  2.1 81.4 %shard_map.73 = bf16[1,1,1,384,1536]{4,3,2,1,0:T(8,128)(2,1)} custom-call(bf16[1,1,1,1,384,1536]{5,4,3,2,1,0:T(8,128)(2,1)} %query.1, bf16[2,1,1,1,1,384,1536]{6,5,4,3,2,1,0:T(8,128)(2,1)} %keyval.1, bf16[1,1,1,1,384,3072]{5,4,3,2,1,0:T(8,128)(2,1)} %hidden.1, bf16[1536,3072]{1,0:T(8,128)(2,1)} %weight.1, f32[1,3072]{1,0:T(1,128)} %gate.1, ...), custom_call_target="tpu_custom_call" | custom-call | tf_op jit(solution)/shard_map/pallas_call | solution.py:422
  83.5 2.4 %copy.11 = bf16[1,1,1,384,1536]{4,3,2,1,0:T(8,128)(2,1)} copy(bf16[1,1,1,384,1536]{4,3,2,1,0:T(8,128)(2,1)} %shard_map.73) | data formatting | bytes 2359296

commit v3 on v2

--- a/solution.py
+++ b/solution.py
@@ -9,9 +9,9 @@
 from jax.sharding import PartitionSpec as P
 
 HEAD_DIM = 128
-GROUP = 2
-DEPTH = 4
-EARLY = 288
+PAIR = 2
+DEPTH = 8
+EARLY = 256
 CHUNKS = 2
 MASKED = -1e30
 MESH = pl.DeviceIdType.MESH
@@ -25,8 +25,8 @@
     a_send, a_recv, p_send, p_recv, x_send, x_recv, kv_sem, q_sem, w_sem, hid_sem, out_sem,
 ):
     rows, channels = query.shape[4], query.shape[5]
-    width = GROUP * HEAD_DIM
-    groups = channels // width
+    heads = channels // HEAD_DIM
+    pairs, width = heads // PAIR, PAIR * HEAD_DIM
     model = hidden.shape[5]
     half = model // 2
     scale = HEAD_DIM**-0.5 * math.log2(math.e)
@@ -39,28 +39,37 @@
     other = {"cfg": 1 - c}
 
     def cols(g):
-        return pl.ds(pl.multiple_of(g * width, width), width)
+        return pl.ds(pl.multiple_of(g * HEAD_DIM, HEAD_DIM), HEAD_DIM)
+
+    def pair_cols(n):
+        return pl.ds(pl.multiple_of(n * width, width), width)
+
+    def kv_slot(slot, g):
+        return kv_buf.at[g, :, pl.ds(pl.multiple_of(slot * rows, rows), rows)]
+
+    def q_slot(slot, g):
+        return q_buf.at[g, pl.ds(pl.multiple_of(slot * rows, rows), rows)]
 
     def kv_local(g):
         return pltpu.make_async_copy(
-            keyval.at[:, 0, 0, 0, 0, :, cols(g)], kv_buf.at[1, g], kv_sem.at[g]
+            keyval.at[:, 0, 0, 0, 0, :, cols(g)], kv_slot(1, g), kv_sem.at[g]
         )
 
     def q_local(g):
         return pltpu.make_async_copy(
-            query.at[0, 0, 0, 0, :, cols(g)], q_buf.at[1, g], q_sem.at[g]
+            query.at[0, 0, 0, 0, :, cols(g)], q_slot(1, g), q_sem.at[g]
         )
 
     middle = times // 2
 
     def relayed(g):
-        return (g == 1) | (g == 2) | (g == 3)
+        return (g >= heads // 6) & (g < heads * 2 // 3)
 
     def kv_copy(side, g):
         by = relayed(g) & (t == (middle, middle - 1)[side])
         return pltpu.make_async_remote_copy(
             keyval.at[:, 0, 0, 0, 0, :, cols(g)],
-            kv_buf.at[jnp.where(by, 2 * side, 2 - 2 * side), g],
+            kv_slot(jnp.where(by, 2 * side, 2 - 2 * side), g),
             kv_send.at[side, g],
             kv_recv.at[jnp.where(by, side, 1 - side), g],
             device_id={"tm": jnp.where(by, (0, times - 1)[side], t + (-1, 1)[side])},
@@ -69,8 +78,8 @@
 
     def kv_forward(side, g):
         return pltpu.make_async_remote_copy(
-            kv_buf.at[2 * side, g],
-            kv_buf.at[2 - 2 * side, g],
+            kv_slot(2 * side, g),
+            kv_slot(2 - 2 * side, g),
             kv_send.at[side, g],
             kv_recv.at[1 - side, g],
             device_id={"tm": (middle - 1, middle)[side]},
@@ -79,8 +88,8 @@
 
     def kv_arrival(side, g):
         return pltpu.make_async_remote_copy(
-            kv_buf.at[2 * side, g],
-            kv_buf.at[2 * side, g],
+            kv_slot(2 * side, g),
+            kv_slot(2 * side, g),
             kv_send.at[side, g],
             kv_recv.at[side, g],
             device_id=other,
@@ -90,7 +99,7 @@
     def q_copy(side, g):
         return pltpu.make_async_remote_copy(
             query.at[0, 0, 0, 0, :, cols(g)],
-            q_buf.at[2 - 2 * side, g],
+            q_slot(2 - 2 * side, g),
             q_send.at[side, g],
             q_recv.at[1 - side, g],
             device_id=(up, down)[side],
@@ -117,12 +126,12 @@
             device_id_type=MESH,
         )
 
-    def a_copy(g):
-        return pltpu.make_async_remote_copy(
-            a_out.at[:, cols(g)],
-            a_in.at[:, cols(g)],
-            a_send.at[g],
-            a_recv.at[g],
+    def a_copy(n):
+        return pltpu.make_async_remote_copy(
+            a_out.at[:, pair_cols(n)],
+            a_in.at[:, pair_cols(n)],
+            a_send.at[n],
+            a_recv.at[n],
             device_id=other,
             device_id_type=MESH,
         )
@@ -159,7 +168,7 @@
 
     w_copy = pltpu.make_async_copy(weight, w_buf, w_sem)
     hid_copy = pltpu.make_async_copy(hidden.at[0, 0, 0, 0], hid_buf, hid_sem)
-    for g in range(groups):
+    for g in range(heads):
         kv_local(g).start()
         q_local(g).start()
 
@@ -201,12 +210,17 @@
 
         @pl.when(jnp.logical_not(has_tm[side]))
         def _():
-            for g in range(groups):
+            for g in range(heads):
                 if not relayed(g):
-                    kv_buf[2 * side, g] = jnp.zeros(kv_buf.shape[2:], kv_buf.dtype)
+                    kv_buf[g, :, 2 * side * rows : (2 * side + 1) * rows] = jnp.zeros(
+                        (2, rows, HEAD_DIM), kv_buf.dtype
+                    )
 
         @pl.when(jnp.logical_not(has_height[side]))
         def _():
+            q_buf[:, 2 * side * rows : (2 * side + 1) * rows] = jnp.zeros(
+                (heads, rows, HEAD_DIM), q_buf.dtype
+            )
             o_in[side] = jnp.zeros(o_in.shape[1:], o_in.dtype)
             l_in[side] = jnp.full(l_in.shape[1:], MASKED, l_in.dtype)
 
@@ -215,103 +229,101 @@
     for step in (-1, 0, 1):
         at = jnp.clip(t + step, 0, times - 1)
         inside = (t + step >= 0) & (t + step < times)
-        live.append(position < jnp.where(inside, counts[at, h, 0], 0))
-    own_count = counts[t, h, 0]
+        seen = position < jnp.where(inside, counts[at, 0, h], 0)
+        live.append(seen.astype(jnp.int32))
+    live = jnp.concatenate(live, axis=1) > 0
+    own_count = counts[t, 0, h]
     query_live = (
         lax.broadcasted_iota(jnp.int32, (rows, HEAD_DIM), 0) < own_count
     ).astype(jnp.float32)
     low_lanes = lax.broadcasted_iota(jnp.int32, (rows, HEAD_DIM), 1) < HEAD_DIM // 2
-    ones = jnp.ones((rows, HEAD_DIM), jnp.bfloat16)
-
-    def attend_head(tile, g, j):
-        at = slice(j * HEAD_DIM, (j + 1) * HEAD_DIM)
-        q = q_buf[tile, g, :, at]
-        scores = []
-        for i in range(3):
-            s = lax.dot_general(
-                q, kv_buf[i, g, 0, :, at], (((1,), (1,)), ((), ())),
-                preferred_element_type=jnp.float32,
-            )
-            scores.append(jnp.where(live[i], s, MASKED))
-        top = jnp.maximum(jnp.maximum(scores[0], scores[1]), scores[2])
-        top = jnp.max(top, axis=1, keepdims=True)
-        mixed = jnp.zeros((rows, 2 * HEAD_DIM), jnp.float32)
-        for i in range(3):
-            p = jnp.exp2((scores[i] - top) * scale).astype(jnp.bfloat16)
-            v = jnp.concatenate([kv_buf[i, g, 1, :, at], ones], axis=1)
-            mixed = mixed + jnp.dot(p, v, preferred_element_type=jnp.float32)
+    ones = jnp.ones((3 * rows, HEAD_DIM), jnp.bfloat16)
+
+    def attend_rows(first, size, g):
+        scores = lax.dot_general(
+            q_buf[g, first : first + size], kv_buf[g, 0], (((1,), (1,)), ((), ())),
+            preferred_element_type=jnp.float32,
+        )
+        scores = jnp.where(live, scores, MASKED)
+        top = jnp.max(scores, axis=1, keepdims=True)
+        probs = jnp.exp2((scores - top) * scale).astype(jnp.bfloat16)
+        values = jnp.concatenate([kv_buf[g, 1], ones], axis=1)
+        mixed = jnp.dot(probs, values, preferred_element_type=jnp.float32)
         total = mixed[:, HEAD_DIM:]
-        result = mixed[:, :HEAD_DIM] / total
-        return result, top * scale + jnp.log(total) * math.log2(math.e)
+        level = top * scale + jnp.log(total) * math.log2(math.e)
+        return mixed[:, :HEAD_DIM] / total, level
 
     def attend(g):
-        def one(tile):
-            heads = [attend_head(tile, g, j) for j in range(GROUP)]
-            mixed = jnp.concatenate([x for x, _ in heads], axis=1)
-            return mixed, jnp.where(low_lanes, heads[0][1], heads[1][1])
-
+        for side in range(2):
+            pl.when(has_height[side])(q_copy(1 - side, g).wait_recv)
+
+        size = 3 * rows // 2
+        results = [attend_rows(first, size, g) for first in (0, size)]
+        mixed = jnp.concatenate([x for x, _ in results], axis=0)
+        level = jnp.concatenate([x for _, x in results], axis=0)
+        for side in range(2):
+            at = slice(2 * side * rows, (2 * side + 1) * rows)
+            o_out[side, g] = mixed[at].astype(jnp.bfloat16)
+            l_out[side, g] = jnp.transpose(level[at])[:8]
+        o_own[g] = mixed[rows : 2 * rows]
+        l_own[g] = level[rows : 2 * rows]
         for side in range(2):
 
             @pl.when(has_height[side])
             def _():
-                q_copy(1 - side, g).wait_recv()
-                mixed, level = one(2 * side)
-                o_out[side, g] = mixed.astype(jnp.bfloat16)
-                l_out[side, g] = level
                 o_copy(side, g).start()
                 l_copy(side, g).start()
 
-        mixed, level = one(1)
-        o_own[g] = mixed
-        l_own[g] = level
-
-    def combine(g):
+    def combine(n):
         for side in range(2):
 
             @pl.when(has_height[side])
             def _():
-                o_copy(1 - side, g).wait_recv()
-                l_copy(1 - side, g).wait_recv()
-
-        levels = [l_in[0, g], l_own[g], l_in[1, g]]
+                for j in range(PAIR):
+                    o_copy(1 - side, n * PAIR + j).wait_recv()
+                    l_copy(1 - side, n * PAIR + j).wait_recv()
+
+        def arrived(side):
+            spread = [
+                jnp.broadcast_to(l_in[side, n * PAIR + j, :1], (HEAD_DIM // 2, rows))
+                for j in range(PAIR)
+            ]
+            return jnp.transpose(jnp.concatenate(spread, axis=0))
+
+        own_level = jnp.where(low_lanes, l_own[n * PAIR], l_own[n * PAIR + 1])
+        levels = [arrived(0), own_level, arrived(1)]
         top = jnp.maximum(jnp.maximum(levels[0], levels[1]), levels[2])
         shares = [jnp.exp2(x - top) for x in levels]
         total = shares[0] + shares[1] + shares[2]
         shares = [x / total * query_live for x in shares]
         parts = []
-        for j in range(GROUP):
-            at = slice(j * HEAD_DIM, (j + 1) * HEAD_DIM)
-            lane = j * HEAD_DIM // 2
+        for j in range(PAIR):
+            lane, g = j * HEAD_DIM // 2, n * PAIR + j
             parts.append(
-                shares[0][:, lane : lane + 1] * o_in[0, g, :, at].astype(jnp.float32)
-                + shares[1][:, lane : lane + 1] * o_own[g, :, at]
-                + shares[2][:, lane : lane + 1] * o_in[1, g, :, at].astype(jnp.float32)
+                shares[0][:, lane : lane + 1] * o_in[0, g].astype(jnp.float32)
+                + shares[1][:, lane : lane + 1] * o_own[g]
+                + shares[2][:, lane : lane + 1] * o_in[1, g].astype(jnp.float32)
             )
         attended = jnp.concatenate(parts, axis=1).astype(jnp.bfloat16)
-        a_out[:, cols(g)] = attended[:EARLY]
-        a_copy(g).start()
-        project(g, attended[EARLY:], acc_late, (1 - c) * half)
-        project(g, attended, acc, c * half)
-
-    def project(g, attended, total, first):
+        a_out[:, pair_cols(n)] = attended[:EARLY]
+        a_copy(n).start()
+        project(n, attended[EARLY:], acc_late, (1 - c) * half)
+        return attended
+
+    def project(n, attended, total, first):
         block = 512
-        depth = pl.ds(pl.multiple_of(g * width, width), width)
-
-        def add(k, carry):
-            at = pl.ds(pl.multiple_of(k * block, block), block)
+        depth = pair_cols(n)
+
+        for k in range(half // block):
+            at = slice(k * block, (k + 1) * block)
             column = pl.ds(pl.multiple_of(first + k * block, block), block)
             total[:, at] += jnp.dot(
                 attended, w_buf[depth, column], preferred_element_type=jnp.float32
             )
-            return carry
-
-        lax.fori_loop(0, half // block, add, 0)
 
     acc_late[...] = jnp.zeros_like(acc_late)
     acc[...] = jnp.zeros_like(acc)
-    w_copy.wait()
-
-    def step(g, carry):
+    def receive(g):
         for side in range(2):
             end = t == (0, times - 1)[side]
             pl.when(has_tm[side])(kv_arrival(side, g).wait_recv)
@@ -324,22 +336,38 @@
         kv_local(g).wait()
         q_local(g).wait()
 
-        @pl.when(g + DEPTH < groups)
+        @pl.when(g + DEPTH < heads)
         def _():
             for side in range(2):
                 pl.when(has_height[side])(q_copy(side, g + DEPTH).start)
                 pl.when(has_tm[side])(kv_copy(side, g + DEPTH).start)
 
-        attend(g)
-
-        @pl.when(g > 0)
+    def step(n, carry):
+        for j in range(PAIR):
+            receive(n * PAIR + j)
+            attend(n * PAIR + j)
+
+        pl.when(n == 1)(w_copy.wait)
+
+        @pl.when(n > 0)
         def _():
-            combine(g - 1)
+            project(n - 1, combine(n - 1), acc, c * half)
 
         return carry
 
-    lax.fori_loop(0, groups, step, 0)
-    combine(groups - 1)
+    lax.fori_loop(0, pairs, step, 0)
+
+    ahead = pairs // 2
+    for n in range(ahead):
+        a_copy(n).wait_recv()
+    block = 512
+    for k in range(half // block):
+        column = pl.ds(pl.multiple_of(c * half + k * block, block), block)
+        acc_in[:, k * block : (k + 1) * block] = jnp.dot(
+            a_in[:, : ahead * width], w_buf[: ahead * width, column],
+            preferred_element_type=jnp.float32,
+        )
+    attended = combine(pairs - 1)
     hid_copy.wait()
     for k in range(CHUNKS):
         piece = slice(k * chunk, (k + 1) * chunk)
@@ -348,18 +376,15 @@
             stream.astype(jnp.float32) + gate[:, theirs] * acc_late[piece]
         ).astype(jnp.bfloat16)
         p_copy(k).start()
-    for g in range(groups):
-        a_copy(g).wait_recv()
-
-    def project_in(k, carry):
-        at = pl.ds(pl.multiple_of(k * 256, 256), 256)
-        column = pl.ds(pl.multiple_of(c * half + k * 256, 256), 256)
-        acc_in[:, at] = jnp.dot(
-            a_in[...], w_buf[:, column], preferred_element_type=jnp.float32
-        )
-        return carry
-
-    lax.fori_loop(0, half // 256, project_in, 0)
+    project(pairs - 1, attended, acc, c * half)
+    for n in range(ahead, pairs):
+        a_copy(n).wait_recv()
+    for k in range(half // block):
+        column = pl.ds(pl.multiple_of(c * half + k * block, block), block)
+        acc_in[:, k * block : (k + 1) * block] += jnp.dot(
+            a_in[:, ahead * width :], w_buf[ahead * width :, column],
+            preferred_element_type=jnp.float32,
+        )
     hid_swap.wait_recv()
     gate_swap.wait_recv()
 
@@ -393,7 +418,6 @@
     gate_swap.wait_send()
 
     def drain(g, carry):
-        a_copy(g).wait_send()
         for side in range(2):
             end = t == (0, times - 1)[side]
             pl.when(has_tm[side])(kv_copy(side, g).wait_send)
@@ -407,14 +431,15 @@
 
         return carry
 
-    lax.fori_loop(0, groups, drain, 0)
+    lax.fori_loop(0, heads, drain, 0)
+    for n in range(pairs):
+        a_copy(n).wait_send()
 
 
 def on_device(query, keyval, hidden, out_weight, gate_scale, guidance, counts):
     rows, channels = query.shape[4], query.shape[5]
     model = hidden.shape[5]
-    width = GROUP * HEAD_DIM
-    groups = channels // width
+    heads = channels // HEAD_DIM
     bf16, f32, dma = jnp.bfloat16, jnp.float32, pltpu.SemaphoreType.DMA
     anywhere = pl.BlockSpec(memory_space=pl.ANY)
     vmem = pl.BlockSpec(memory_space=pltpu.VMEM)
@@ -425,16 +450,16 @@
         in_specs=[anywhere, anywhere, anywhere, anywhere, vmem, smem, smem],
         out_specs=anywhere,
         scratch_shapes=[
-            pltpu.VMEM((3, groups, rows, width), bf16),
-            pltpu.VMEM((3, groups, 2, rows, width), bf16),
+            pltpu.VMEM((heads, 3 * rows, HEAD_DIM), bf16),
+            pltpu.VMEM((heads, 2, 3 * rows, HEAD_DIM), bf16),
             pltpu.VMEM((channels, model), bf16),
             pltpu.VMEM((rows, model), bf16),
-            pltpu.VMEM((groups, rows, width), f32),
-            pltpu.VMEM((2, groups, rows, width), bf16),
-            pltpu.VMEM((2, groups, rows, width), bf16),
-            pltpu.VMEM((groups, rows, HEAD_DIM), f32),
-            pltpu.VMEM((2, groups, rows, HEAD_DIM), f32),
-            pltpu.VMEM((2, groups, rows, HEAD_DIM), f32),
+            pltpu.VMEM((heads, rows, HEAD_DIM), f32),
+            pltpu.VMEM((2, heads, rows, HEAD_DIM), bf16),
+            pltpu.VMEM((2, heads, rows, HEAD_DIM), bf16),
+            pltpu.VMEM((heads, rows, HEAD_DIM), f32),
+            pltpu.VMEM((2, heads, 8, rows), f32),
+            pltpu.VMEM((2, heads, 8, rows), f32),
             pltpu.VMEM((rows, model // 2), f32),
             pltpu.VMEM((rows - EARLY, model // 2), f32),
             pltpu.VMEM((EARLY, model // 2), f32),
@@ -446,16 +471,16 @@
             pltpu.VMEM((1, model), f32),
             pltpu.VMEM((rows, model // 2), bf16),
         ]
-        + [dma((2, groups))] * 8
-        + [dma((groups,))] * 2
+        + [dma((2, heads))] * 8
+        + [dma((heads // PAIR,))] * 2
         + [dma((CHUNKS,))] * 2
         + [dma((2,))] * 2
-        + [dma((groups,))] * 2
+        + [dma((heads,))] * 2
         + [dma, dma, dma((rows * CHUNKS // (rows - EARLY),))],
         compiler_params=pltpu.CompilerParams(
             collective_id=0, has_side_effects=True, vmem_limit_bytes=60 * 2**20
         ),
-    )(query, keyval, hidden, out_weight, gate_scale, guidance, counts)
+    )(query, keyval, hidden, out_weight, gate_scale, guidance, jnp.swapaxes(counts, 1, 2))
 
 
 def solution(mesh):

time: 86.6 us -> 84.4 us (0.975)
  local copies, waits for them, and re-layouts: 3.78 us -> 2.36 us
    unnamed x2 -> x1, local copies, waits for them, and re-layouts: 3.78 us -> 2.36 us
where the time goes in v3:
time: 84.4 us; the launch traced here: 83.9 us
  Pallas kernels  80.9 us (96%)
  local copies, waits for them, and re-layouts  2.36 us (3%)
    pallas_call x1, Pallas kernels, on_device(): pl.pallas_call(kernel, out_shape=jax.ShapeDtypeStruct((1, 1, 1, rows, mod...  80.9 us
    unnamed x1, local copies, waits for them, and re-layouts  2.36 us

profile of v3, /device:TPU:11, one launch (start us, length us, event | category | flops | bytes accessed | tf_op | source)
XLA Modules:
  0.0 83.9 jit_solution(4831803825467878432)
XLA Ops:
  0.7 80.9 %shard_map.73 = bf16[1,1,1,384,1536]{4,3,2,1,0:T(8,128)(2,1)} custom-call(bf16[1,1,1,1,384,1536]{5,4,3,2,1,0:T(8,128)(2,1)} %query.1, bf16[2,1,1,1,1,384,1536]{6,5,4,3,2,1,0:T(8,128)(2,1)} %keyval.1, bf16[1,1,1,1,384,3072]{5,4,3,2,1,0:T(8,128)(2,1)} %hidden.1, bf16[1536,3072]{1,0:T(8,128)(2,1)} %weight.1, f32[1,3072]{1,0:T(1,128)} %gate.1, ...), custom_call_target="tpu_custom_call" | custom-call | tf_op jit(solution)/shard_map/pallas_call | solution.py:447
  81.5 2.4 %copy.11 = bf16[1,1,1,384,1536]{4,3,2,1,0:T(8,128)(2,1)} copy(bf16[1,1,1,384,1536]{4,3,2,1,0:T(8,128)(2,1)} %shard_map.73) | data formatting | bytes 2359296

commit v4 on v3

--- a/solution.py
+++ b/solution.py
@@ -343,15 +343,17 @@
                 pl.when(has_tm[side])(kv_copy(side, g + DEPTH).start)
 
     def step(n, carry):
-        for j in range(PAIR):
-            receive(n * PAIR + j)
-            attend(n * PAIR + j)
-
+        receive(n * PAIR)
+        attend(n * PAIR)
         pl.when(n == 1)(w_copy.wait)
 
         @pl.when(n > 0)
         def _():
             project(n - 1, combine(n - 1), acc, c * half)
+
+        for j in range(1, PAIR):
+            receive(n * PAIR + j)
+            attend(n * PAIR + j)
 
         return carry
 

time: 84.4 us -> 84.4 us (level)
  no operation moved by 1% of the time
where the time goes in v4:
time: 84.4 us; the launch traced here: 84.3 us
  Pallas kernels  81.2 us (96%)
  local copies, waits for them, and re-layouts  2.36 us (3%)
    pallas_call x1, Pallas kernels, on_device(): pl.pallas_call(kernel, out_shape=jax.ShapeDtypeStruct((1, 1, 1, rows, mod...  81.2 us
    unnamed x1, local copies, waits for them, and re-layouts  2.36 us

profile of v4, /device:TPU:11, one launch (start us, length us, event | category | flops | bytes accessed | tf_op | source)
XLA Modules:
  0.0 84.3 jit_solution(6152690171358254679)
XLA Ops:
  0.7 81.2 %shard_map.73 = bf16[1,1,1,384,1536]{4,3,2,1,0:T(8,128)(2,1)} custom-call(bf16[1,1,1,1,384,1536]{5,4,3,2,1,0:T(8,128)(2,1)} %query.1, bf16[2,1,1,1,1,384,1536]{6,5,4,3,2,1,0:T(8,128)(2,1)} %keyval.1, bf16[1,1,1,1,384,3072]{5,4,3,2,1,0:T(8,128)(2,1)} %hidden.1, bf16[1536,3072]{1,0:T(8,128)(2,1)} %weight.1, f32[1,3072]{1,0:T(1,128)} %gate.1, ...), custom_call_target="tpu_custom_call" | custom-call | tf_op jit(solution)/shard_map/pallas_call | solution.py:449
  81.9 2.4 %copy.11 = bf16[1,1,1,384,1536]{4,3,2,1,0:T(8,128)(2,1)} copy(bf16[1,1,1,384,1536]{4,3,2,1,0:T(8,128)(2,1)} %shard_map.73) | data formatting | bytes 2359296
